TPU v7x, 32 devices: a whole 2x2x4 slice. The times are simulated.
32 devices in a mesh: pole: 2 (over y), prow: 4 (over z), pcol: 4 (over x, core).
Axes of the slice: x: 2, y: 2, z: 4, core: 2. Of those that a mesh axis runs over, the one named last changes fastest.
Arguments:
- ginv: bfloat16 [4096, 2048], P(('pole', 'prow'), 'pcol'), parts along dimension 0, may hold values from -6 to 6
- panels: bfloat16 [8, 1024, 256], P('pole', 'prow'), parts along dimension 0, may hold values from -0.1875 to 0.1875
- structure: int32 [4, 4], replicated, may hold values from 0 to 7, all different within a row
- dinv: float32 [8, 256, 256], P('pole'), parts along dimension 0, may hold values from -6 to 6
Outputs:
- offdiag: float32 [4096, 1024], P(('pole', 'prow', 'pcol')), parts along dimension 0
- diag: float32 [8, 256, 256], P('pole'), parts along dimension 0
There are 2 independent parts, one for each index of `pole`. A program takes and returns all parts, laid end to end along the dimension named above; an argument that names none is the same for every part. Nothing has to cross between parts.
Inputs may be any that keep to these rules, and one draw needn't show every extreme that they name: `structure`: each row names 4 different ancestor supernodes, and every ancestor supernode is named by some row.
All inputs are finite; a program needn't handle non-finite values.
Results may differ from a plain program's by a relative error of at most 0.0003.
Values may be sent and summed in bfloat16 or wider, within the bound.
A program may use at most 128 MiB of HBM per device.

v0:
```python
import jax
import jax.numpy as jnp
from jax import lax
from jax.sharding import PartitionSpec as P


def pick_blocks(structure, blocks, first_block, block_count):
    targets = first_block + jnp.arange(block_count, dtype=jnp.int32)
    onehot = (structure[:, None, :] == targets[None, :, None]).astype(jnp.bfloat16)
    picked = jnp.einsum("sjp,spab->jasb", onehot, blocks, preferred_element_type=jnp.float32)
    return picked.astype(jnp.bfloat16)


def contract(left_rows, right_rows, super_count, block_width):
    left_cube = left_rows.astype(jnp.float32).reshape(left_rows.shape[0], super_count, block_width)
    right_cube = right_rows.reshape(right_rows.shape[0], super_count, block_width)
    return jnp.einsum("ksa,ksb->sab", left_cube, right_cube, precision=lax.Precision.HIGHEST)


def per_device(ginv, panels, structure, dinv):
    super_count = panels.shape[0]
    block_width = panels.shape[2]
    struct_count = structure.shape[1]
    col_parts = lax.axis_size("pcol")
    row_rank = lax.axis_index("prow")
    col_rank = lax.axis_index("pcol")
    local_rows = ginv.shape[0]
    row_blocks = local_rows // block_width
    col_blocks = ginv.shape[1] // block_width
    keep_rows = local_rows // col_parts
    gathered = lax.all_gather(panels, "prow", axis=1, tiled=True)
    blocks = gathered.reshape(super_count, struct_count, block_width, block_width)
    column_sel = pick_blocks(structure, blocks, col_rank * col_blocks, col_blocks)
    row_sel = pick_blocks(structure, blocks, row_rank * row_blocks, row_blocks)
    column_mat = column_sel.reshape(col_blocks * block_width, super_count * block_width)
    row_mat = row_sel.reshape(local_rows, super_count * block_width)
    summed = lax.psum_scatter(
        jnp.dot(ginv, column_mat, preferred_element_type=jnp.float32),
        "pcol",
        scatter_dimension=0,
        tiled=True,
    )
    own_rows = lax.dynamic_slice_in_dim(row_mat, col_rank * keep_rows, keep_rows, 0)
    diag_terms = contract(own_rows, summed, super_count, block_width)
    diag_total = lax.psum(diag_terms, ("prow", "pcol"))
    return (-summed, dinv + diag_total)


def solution(mesh):
    return jax.shard_map(
        per_device,
        mesh=mesh,
        in_specs=(P(("pole", "prow"), "pcol"), P("pole", "prow", None), P(), P("pole", None, None)),
        out_specs=(P(("pole", "prow", "pcol"), None), P("pole", None, None)),
        check_vma=False,
    )
```

profile of v0, /device:TPU:1, one launch (start us, length us, event | category | flops | bytes accessed | tf_op | source)
XLA Modules:
  0.0 200.4 jit_solution(9070442356904195712)
XLA Ops:
  7.2 0.0 copy-start
  7.2 0.0 all-gather.2.cloned.1.call-start
  7.2 0.7 all-gather.2.cloned.1.call-update
  7.9 0.0 reduce-scatter.2.cloned.1.call-start
  8.0 49.6 %all-gather.2.cloned.1.call-done = bf16[4,1024,256]{2,1,0:T(8,128)(2,1)} async-done(((bf16[4,256,256]{2,1,0:T(8,128)(2,1)}), bf16[4,1024,256]{2,1,0:T(8,128)(2,1)}) %all-gather.2.cloned.1.call-update) | async-done | bytes 2097168 | tf_op jit(solution)/shard_map/all_gather | solution.py:31
  57.6 3.4 %fusion.13 = bf16[2,256,4,256]{3,0,1,2:T(2,128)(2,1)S(1)} fusion(bf16[4,4,256,256]{3,2,1,0:T(8,128)(2,1)} %bitcast.35, s32[4,4]{1,0:T(4,128)} %param.6, s32[2]{0:T(128)S(1)} %iota_add_fusion.1), kind=kOutput, calls=%fused_computation.8 | convolution fusion | flops 4718624 | bytes 3145800 | tf_op jit(solution)/shard_map/sjp,spab->jasb/dot_general | solution.py:10
  61.0 0.8 copy.9
  61.8 0.2 copy.18
  62.0 0.0 copy-start.4
  62.1 2.1 %convolution_bitcast_fusion = f32[512,1024]{0,1:T(8,128)} fusion(bf16[512,1024]{1,0:T(8,128)(2,1)S(1)} %bitcast.29, bf16[512,512]{1,0:T(8,128)(2,1)S(1)} %copy-done), kind=kOutput, calls=%fused_computation | convolution fusion | flops 536870912 | bytes 3670016 | tf_op jit(solution)/shard_map/dot_general | solution.py:38
  64.1 0.0 reduce-scatter.2.cloned.1.call-update
  64.1 0.0 all-reduce.2.cloned.1.call-start
  64.2 0.0 copy-done.3
  64.2 0.0 copy-done.4
  64.2 1.8 fusion.10
  66.0 0.8 copy.11
  66.8 0.2 copy.19
  67.1 0.2 copy.12
  67.3 27.2 %reduce-scatter.2.cloned.1.call-done = f32[128,1024]{0,1:T(8,128)} async-done(((f32[512,1024]{0,1:T(8,128)}), f32[128,1024]{0,1:T(8,128)}) %reduce-scatter.2.cloned.1.call-update) | async-done | bytes 524304 | tf_op jit(solution)/shard_map/reduce_scatter | solution.py:37
  94.5 2.7 %fusion.24 = f32[4,256,256]{2,1,0:T(8,128)} fusion(bf16[128,4,256]{0,2,1:T(8,128)(2,1)S(1)} %bitcast.34, f32[128,4,256]{0,2,1:T(8,128)} %bitcast.32), kind=kOutput, calls=%fused_computation.20 | convolution fusion | flops 402653184 | bytes 1835008 | tf_op jit(solution)/shard_map/ksa,ksb->sab/dot_general | solution.py:17
  97.2 0.0 all-reduce.2.cloned.1.call-update
  97.3 1.0 copy.14
  98.3 93.3 %all-reduce.2.cloned.1.call-done = f32[4,256,256]{2,1,0:T(8,128)} async-done(((f32[4,256,256]{2,1,0:T(8,128)}), f32[4,256,256]{2,1,0:T(8,128)}) %all-reduce.2.cloned.1.call-update) | async-done | bytes 1048592 | tf_op jit(solution)/shard_map/psum | solution.py:45
  191.6 2.3 %add.35 = f32[4,256,256]{2,1,0:T(8,128)} add(f32[4,256,256]{2,1,0:T(8,128)S(1)} %copy-done.2, f32[4,256,256]{2,1,0:T(8,128)} %all-reduce.2.cloned.1.call-done) | non-fusion elementwise | flops 262144 | bytes 3145728 | tf_op jit(solution)/shard_map/add | solution.py:46
  (10 shorter events, 0.1 us)
Async XLA Ops:
  7.2 54.9 %copy-start = (bf16[512,512]{1,0:T(8,128)(2,1)S(1)}, bf16[512,512]{1,0:T(8,128)(2,1)}, u32[]{:S(2)}) copy-start(bf16[512,512]{1,0:T(8,128)(2,1)} %param.4) | copy-start | bytes 1572868
  7.2 50.4 %all-gather.2.cloned.1.call-start = ((), (), s32[]{:S(2)}) async-start(), calls=%async_computation.1 | async-start | bytes 2621440 | tf_op jit(solution)/shard_map/all_gather | solution.py:31
  7.9 86.6 %reduce-scatter.2.cloned.1.call-start = ((), (), s32[]{:S(2)}) async-start(), calls=%async_computation.2 | async-start | bytes 2621440 | tf_op jit(solution)/shard_map/reduce_scatter | solution.py:37
  62.0 2.2 %copy-start.3 = (bf16[4,1024,256]{2,1,0:T(8,128)(2,1)S(1)}, bf16[4,1024,256]{2,1,0:T(8,128)(2,1)}, u32[]{:S(2)}) copy-start(bf16[4,1024,256]{2,1,0:T(8,128)(2,1)} %all-gather.2.cloned.1.call-done) | copy-start | bytes 6291460
  62.0 2.2 %copy-start.4 = (s32[4,4]{1,0:T(4,128)S(1)}, s32[4,4]{1,0:T(4,128)}, u32[]{:S(2)}) copy-start(s32[4,4]{1,0:T(4,128)} %param.6) | copy-start | bytes 196
  64.1 127.4 %all-reduce.2.cloned.1.call-start = ((), (), s32[]{:S(2)}) async-start(), calls=%async_computation.3 | async-start | bytes 2097152 | tf_op jit(solution)/shard_map/psum | solution.py:45
  94.5 2.8 %copy-start.1 = (f32[128,1024]{0,1:T(8,128)S(1)}, f32[128,1024]{0,1:T(8,128)}, u32[]{:S(2)}) copy-start(f32[128,1024]{0,1:T(8,128)} %reduce-scatter.2.cloned.1.call-done) | copy-start | bytes 1572868
  94.5 97.1 %copy-start.2 = (f32[4,256,256]{2,1,0:T(8,128)S(1)}, f32[4,256,256]{2,1,0:T(8,128)}, u32[]{:S(2)}) copy-start(f32[4,256,256]{2,1,0:T(8,128)} %param.7) | copy-start | bytes 3145732
Sparse Core Ops, SparseCore 0:
  9.6 47.9 all-gather.1
  64.3 30.1 reduce-scatter.1
  98.9 92.5 all-reduce.1
where the time goes:
time: 202 us; the launch traced here: 200 us
  waiting for transfers between devices  171 us (85%)
  between operations  13.9 us (7%)
  matrix products  9.93 us (5%)
  local copies, waits for them, and re-layouts  3.28 us (2%)
  other arithmetic  2.37 us (1%)
    psum x1, waiting for transfers between devices, per_device(): diag_total = lax.psum(diag_terms, ('prow', 'pcol'))  93.3 us
    all_gather x1, waiting for transfers between devices, per_device(): gathered = lax.all_gather(panels, 'prow', axis=1, tiled=True)  49.6 us
    reduce_scatter x1, waiting for transfers between devices, per_device(): lax.psum_scatter(jnp.dot(ginv, column_mat, preferred_element_type=jnp.flo...  27.2 us
    dot_general x2, matrix products, pick_blocks(): jnp.einsum('sjp,spab->jasb', onehot, blocks, preferred_element_type=jnp.f...  5.14 us
  transfers between devices with their start and end apart: 3, of which 3 were waited for; matrix products, arithmetic and copies ran while one was open for 2% of the time, Pallas kernels for 0%

commit v1 on v0

v1 whole, which is shorter than its diff:
```python
import functools

import jax
import jax.numpy as jnp
from jax import lax
from jax.experimental import pallas as pl
from jax.experimental.pallas import tpu as pltpu
from jax.sharding import PartitionSpec as P

MESH = pl.DeviceIdType.MESH
VMEM_BYTES = 48 * 1024 * 1024


def invert_kernel(
    nz, ginv_ref, panels_ref, struct_ref, dinv_ref, off_ref, diag_ref,
    g_buf, p_buf, prod, part, rs_buf, dinv_buf,
    p_send, p_recv, g_send, g_recv, o_send, o_recv,
    r_send, r_recv, a_send, a_recv, h_send, h_recv, d_sem,
):
    z = lax.axis_index("prow")
    c = lax.axis_index("pcol")
    x, k = c // 2, c % 2
    sib, nbr, dia = 2 * x + 1 - k, 2 * (1 - x) + k, 2 * (1 - x) + 1 - k
    width = panels_ref.shape[2]
    rows, cols = ginv_ref.shape
    col_blocks, row_blocks = cols // width, rows // width
    struct_count = struct_ref.shape[1]
    keep = off_ref.shape[0]
    piece = part.shape[0] // nz

    def zat(d):
        return lax.rem(z + d, nz)

    def zfrom(d):
        return lax.rem(z + nz - d, nz)

    def remote(src, dst, send, recv, zt, ct):
        return pltpu.make_async_remote_copy(
            src_ref=src, dst_ref=dst, send_sem=send, recv_sem=recv,
            device_id={"prow": zt, "pcol": ct}, device_id_type=MESH,
        )

    dinv_copy = pltpu.make_async_copy(dinv_ref.at[c, pl.ds(z * piece, piece)], dinv_buf, d_sem)
    dinv_copy.start()

    barrier = pltpu.get_barrier_semaphore()
    for d in range(1, nz):
        pl.semaphore_signal(barrier, inc=1, device_id={"prow": zat(d), "pcol": c}, device_id_type=MESH)
    for ct in (sib, nbr, dia):
        pl.semaphore_signal(barrier, inc=1, device_id={"prow": z, "pcol": ct}, device_id_type=MESH)
    pl.semaphore_wait(barrier, nz + 2)

    g_nbr, g_sib, g_fwd, panel_copies = [], [], [], []
    for h in range(col_blocks):
        src = ginv_ref.at[:, pl.ds(h * width, width)]
        dst = g_buf.at[c * col_blocks + h]
        g_nbr.append(remote(src, dst, g_send.at[0, h], g_recv.at[0, h], z, nbr))
        g_sib.append(remote(src, dst, g_send.at[1, h], g_recv.at[1, h], z, sib))
        held = g_buf.at[nbr * col_blocks + h]
        g_fwd.append(remote(held, held, g_send.at[2, h], g_recv.at[2, h], z, sib))
    for d in range(1, nz):
        panel_copies.append(
            remote(panels_ref.at[c], p_buf.at[z], p_send.at[d - 1], p_recv.at[d - 1], zat(d), c)
        )
    for copy in g_nbr + panel_copies + g_sib:
        copy.start()
    p_buf[z] = panels_ref[c]
    for h in range(col_blocks):
        g_buf[c * col_blocks + h] = ginv_ref[:, h * width:(h + 1) * width]
    for h in range(col_blocks):
        g_nbr[h].wait_recv()
        g_fwd[h].start()
    for copy in panel_copies + g_sib + g_fwd:
        copy.wait_recv()

    for at in range(0, rows, keep):
        acc = jnp.zeros((keep, width), jnp.float32)
        for p in range(struct_count):
            acc += jnp.dot(
                g_buf[struct_ref[c, p], pl.ds(at, keep), :], p_buf[p],
                preferred_element_type=jnp.float32,
            )
        prod[at:at + keep, :] = acc

    own_cols = pl.ds(pl.multiple_of(c * width, width), width)
    off_copies = []
    for at, ct in enumerate((nbr, dia, sib)):
        off_copies.append(
            remote(prod.at[pl.ds(ct * keep, keep)], off_ref.at[:, own_cols], o_send.at[at], o_recv.at[at], z, ct)
        )

    total = jnp.zeros((width, width), jnp.float32)
    for b in range(row_blocks):
        target = z * row_blocks + b
        place, named = jnp.int32(0), jnp.int32(0)
        for p in range(struct_count):
            hit = struct_ref[c, p] == target
            place = jnp.where(hit, p, place)
            named = jnp.where(hit, 1, named)
        right = prod[b * width:(b + 1) * width, :]
        high = right.astype(jnp.bfloat16)
        low = (right - high.astype(jnp.float32)).astype(jnp.bfloat16)
        left = p_buf[place]
        contract = (((0,), (0,)), ((), ()))
        term = lax.dot_general(left, high, contract, preferred_element_type=jnp.float32)
        term += lax.dot_general(left, low, contract, preferred_element_type=jnp.float32)
        total += term * named.astype(jnp.float32)
    part[...] = total

    sum_copies = []
    for d in range(1, nz):
        sum_copies.append(
            remote(part.at[pl.ds(zat(d) * piece, piece)], rs_buf.at[d - 1], r_send.at[d - 1], r_recv.at[d - 1], zat(d), c)
        )
    for copy in sum_copies + off_copies:
        copy.start()
    off_ref[:, own_cols] = prod[pl.ds(c * keep, keep), :]

    dinv_copy.wait()
    final = dinv_buf[...] + part[pl.ds(z * piece, piece), :]
    for d in range(1, nz):
        sum_copies[d - 1].wait_recv()
        final += rs_buf[d - 1]
    diag_ref[c, pl.ds(z * piece, piece), :] = final

    over_z, over_x, over_k, over_f = [], [], [], []
    for d in range(nz):
        mine = diag_ref.at[c, pl.ds(zfrom(d) * piece, piece)]
        theirs = diag_ref.at[nbr, pl.ds(zfrom(d) * piece, piece)]
        if d > 0:
            own = diag_ref.at[c, pl.ds(z * piece, piece)]
            over_z.append(remote(own, own, a_send.at[d - 1], a_recv.at[d - 1], zat(d), c))
        over_x.append(remote(mine, mine, h_send.at[0, d], h_recv.at[0, d], z, nbr))
        over_k.append(remote(mine, mine, h_send.at[1, d], h_recv.at[1, d], z, sib))
        over_f.append(remote(theirs, theirs, h_send.at[2, d], h_recv.at[2, d], z, sib))
    for copy in over_z:
        copy.start()
    for d in range(nz):
        if d > 0:
            over_z[d - 1].wait_recv()
        over_x[d].start()
        over_k[d].start()
    for d in range(nz):
        over_x[d].wait_recv()
        over_f[d].start()
    for copy in off_copies + over_k + over_f:
        copy.wait_recv()
    for copy in g_nbr + g_sib + g_fwd + panel_copies + off_copies + sum_copies + over_z + over_x + over_k + over_f:
        copy.wait_send()


def per_device(ginv, panels, structure, dinv):
    super_count, _, width = panels.shape
    nz, nc = lax.axis_size("prow"), lax.axis_size("pcol")
    rows, cols = ginv.shape
    struct_count = structure.shape[1]
    col_blocks = cols // width
    piece = width // nz
    vmem = pl.BlockSpec(memory_space=pltpu.VMEM)
    dma = pltpu.SemaphoreType.DMA
    off, diag = pl.pallas_call(
        functools.partial(invert_kernel, nz),
        out_shape=(
            jax.ShapeDtypeStruct((rows // nc, super_count * width), jnp.float32),
            jax.ShapeDtypeStruct((super_count, width, width), jnp.float32),
        ),
        in_specs=[vmem, vmem, pl.BlockSpec(memory_space=pltpu.SMEM), pl.BlockSpec(memory_space=pl.ANY)],
        out_specs=(vmem, vmem),
        scratch_shapes=[
            pltpu.VMEM((nc * col_blocks, rows, width), jnp.bfloat16),
            pltpu.VMEM((struct_count, width, width), jnp.bfloat16),
            pltpu.VMEM((rows, width), jnp.float32),
            pltpu.VMEM((width, width), jnp.float32),
            pltpu.VMEM((nz - 1, piece, width), jnp.float32),
            pltpu.VMEM((piece, width), jnp.float32),
            dma((nz - 1,)), dma((nz - 1,)),
            dma((3, col_blocks)), dma((3, col_blocks)),
            dma((3,)), dma((3,)),
            dma((nz - 1,)), dma((nz - 1,)),
            dma((nz - 1,)), dma((nz - 1,)),
            dma((3, nz)), dma((3, nz)),
            dma,
        ],
        compiler_params=pltpu.CompilerParams(
            collective_id=0, has_side_effects=True, vmem_limit_bytes=VMEM_BYTES
        ),
        name="selected_inverse",
    )(ginv, panels, structure, dinv)
    return -off, diag


def solution(mesh):
    return jax.shard_map(
        per_device,
        mesh=mesh,
        in_specs=(P(("pole", "prow"), "pcol"), P("pole", "prow", None), P(), P("pole", None, None)),
        out_specs=(P(("pole", "prow", "pcol"), None), P("pole", None, None)),
        check_vma=False,
    )
```

time: 202 us -> 46.1 us (0.23)
  waiting for transfers between devices: 171 us -> 0 us
  Pallas kernels: 0 us -> 39.3 us
  between operations: 13.9 us -> 0.65 us
  matrix products: 9.93 us -> 0 us
    psum x1 -> x0, waiting for transfers between devices: 93.3 us -> none  [per_device(): diag_total = lax.psum(diag_terms, ('prow', 'pcol'))]
    all_gather x1 -> x0, waiting for transfers between devices: 49.6 us -> none  [per_device(): gathered = lax.all_gather(panels, 'prow', axis=1, tiled=True)]
    pallas_call x0 -> x1, Pallas kernels: none -> 39.3 us  [per_device(): pl.pallas_call(functools.partial(invert_kernel, nz), out_shape=(jax.Shape...]
    reduce_scatter x1 -> x0, waiting for transfers between devices: 27.2 us -> none  [per_device(): lax.psum_scatter(jnp.dot(ginv, column_mat, preferred_element_type=jnp.flo...]
    dot_general x4 -> x0, matrix products: 9.93 us -> none  [the longest x2 5.14 us: pick_blocks(): jnp.einsum('sjp,spab->jasb', onehot, blocks, preferred_element_type=jnp.f...]
    unnamed x13 -> x9, local copies, waits for them, and re-layouts: 1.46 us -> 4.95 us
    add x3 -> x0, other arithmetic: 2.34 us -> none  [the longest x1 2.33 us: per_device(): return (-summed, dinv + diag_total)]
  transfers between devices with their start and end apart: 3 -> 0, of which waited for: 3 -> 0; matrix products, arithmetic and copies ran while one was open for 2% -> 0% of each run, Pallas kernels for 0% -> 0%
where the time goes in v1:
time: 46.1 us; the launch traced here: 45.8 us
  Pallas kernels  39.3 us (85%)
  local copies, waits for them, and re-layouts  4.95 us (11%)
  other arithmetic  0.83 us (2%)
  between operations  0.65 us (1%)
    pallas_call x1, Pallas kernels, per_device(): pl.pallas_call(functools.partial(invert_kernel, nz), out_shape=(jax.Shape...  39.3 us
    unnamed x9, local copies, waits for them, and re-layouts  4.95 us

profile of v1, /device:TPU:1, one launch (start us, length us, event | category | flops | bytes accessed | tf_op | source)
XLA Modules:
  0.0 45.8 jit_solution(14816679624216989247)
XLA Ops:
  0.6 0.0 copy-start
  0.6 1.2 %copy-done = f32[4,256,256]{2,1,0:T(8,128)S(1)} copy-done((f32[4,256,256]{2,1,0:T(8,128)S(1)}, f32[4,256,256]{2,1,0:T(8,128)}, u32[]{:S(2)}) %copy-start) | copy-done | bytes 1048600
  1.9 0.0 copy-start.1
  1.9 1.0 %copy-done.1 = bf16[512,512]{1,0:T(8,128)(2,1)S(1)} copy-done((bf16[512,512]{1,0:T(8,128)(2,1)S(1)}, bf16[512,512]{1,0:T(8,128)(2,1)}, u32[]{:S(2)}) %copy-start.1) | copy-done | bytes 524312
  2.9 0.0 copy-start.2
  2.9 1.0 %copy-done.2 = bf16[4,256,256]{2,1,0:T(8,128)(2,1)S(1)} copy-done((bf16[4,256,256]{2,1,0:T(8,128)(2,1)S(1)}, bf16[4,256,256]{2,1,0:T(8,128)(2,1)}, u32[]{:S(2)}) %copy-start.2) | copy-done | bytes 524312
  3.9 0.0 copy-start.3
  3.9 0.7 %copy-done.3 = s32[4,4]{1,0:T(4,128)S(1)} copy-done((s32[4,4]{1,0:T(4,128)S(1)}, s32[4,4]{1,0:T(4,128)}, u32[]{:S(2)}) %copy-start.3) | copy-done | bytes 88
  4.6 39.3 %selected_inverse.1 = (f32[128,1024]{1,0:T(8,128)S(1)}, f32[4,256,256]{2,1,0:T(8,128)S(1)}) custom-call(bf16[512,512]{1,0:T(8,128)(2,1)S(1)} %copy-done.1, bf16[4,256,256]{2,1,0:T(8,128)(2,1)S(1)} %copy-done.2, s32[4,4]{1,0:T(4,128)S(1)} %copy-done.3, f32[4,256,256]{2,1,0:T(8,128)S(1)} %copy-done), custom_call_target="tpu_custom_call" | custom-call | tf_op jit(solution)/shard_map/selected_inverse/pallas_call | solution.py:161
  44.0 0.8 %neg.3 = f32[128,1024]{1,0:T(8,128)} negate(f32[128,1024]{1,0:T(8,128)S(1)} %get-tuple-element.4) | non-fusion elementwise | flops 131072 | bytes 1048576 | tf_op jit(solution)/shard_map/neg | solution.py:189
  44.8 1.0 %copy.7 = f32[4,256,256]{2,1,0:T(8,128)} copy(f32[4,256,256]{2,1,0:T(8,128)S(1)} %get-tuple-element.9) | data formatting | bytes 2097152
Async XLA Ops:
  0.6 1.2 %copy-start = (f32[4,256,256]{2,1,0:T(8,128)S(1)}, f32[4,256,256]{2,1,0:T(8,128)}, u32[]{:S(2)}) copy-start(f32[4,256,256]{2,1,0:T(8,128)} %dinv_ref.1) | copy-start | bytes 3145732
  1.9 1.0 %copy-start.1 = (bf16[512,512]{1,0:T(8,128)(2,1)S(1)}, bf16[512,512]{1,0:T(8,128)(2,1)}, u32[]{:S(2)}) copy-start(bf16[512,512]{1,0:T(8,128)(2,1)} %ginv_ref.1) | copy-start | bytes 1572868
  2.9 1.0 %copy-start.2 = (bf16[4,256,256]{2,1,0:T(8,128)(2,1)S(1)}, bf16[4,256,256]{2,1,0:T(8,128)(2,1)}, u32[]{:S(2)}) copy-start(bf16[4,256,256]{2,1,0:T(8,128)(2,1)} %panels_ref.1) | copy-start | bytes 1572868
  3.9 0.7 %copy-start.3 = (s32[4,4]{1,0:T(4,128)S(1)}, s32[4,4]{1,0:T(4,128)}, u32[]{:S(2)}) copy-start(s32[4,4]{1,0:T(4,128)} %struct_ref.1) | copy-start | bytes 196

commit v2 on v1

--- a/solution.py
+++ b/solution.py
@@ -8,14 +8,14 @@
 from jax.sharding import PartitionSpec as P
 
 MESH = pl.DeviceIdType.MESH
-VMEM_BYTES = 48 * 1024 * 1024
+VMEM_BYTES = 60 * 1024 * 1024
 
 
 def invert_kernel(
-    nz, ginv_ref, panels_ref, struct_ref, dinv_ref, off_ref, diag_ref,
-    g_buf, p_buf, prod, part, rs_buf, dinv_buf,
+    nz, ginv_ref, panels_ref, struct_hbm, dinv_ref, off_hbm, diag_hbm,
+    struct_ref, g_buf, p_buf, prod, neg, part, rs_buf, dinv_buf, off_ref, diag_ref,
     p_send, p_recv, g_send, g_recv, o_send, o_recv,
-    r_send, r_recv, a_send, a_recv, h_send, h_recv, d_sem,
+    r_send, r_recv, a_send, a_recv, h_send, h_recv, l_sem,
 ):
     z = lax.axis_index("prow")
     c = lax.axis_index("pcol")
@@ -40,8 +40,14 @@
             device_id={"prow": zt, "pcol": ct}, device_id_type=MESH,
         )
 
-    dinv_copy = pltpu.make_async_copy(dinv_ref.at[c, pl.ds(z * piece, piece)], dinv_buf, d_sem)
-    dinv_copy.start()
+    dinv_copy = pltpu.make_async_copy(dinv_ref.at[c, pl.ds(z * piece, piece)], dinv_buf, l_sem.at[0])
+    struct_copy = pltpu.make_async_copy(struct_hbm, struct_ref, l_sem.at[1])
+    own_copies = [pltpu.make_async_copy(panels_ref.at[c], p_buf.at[z], l_sem.at[2])]
+    for h in range(col_blocks):
+        src = ginv_ref.at[:, pl.ds(h * width, width)]
+        own_copies.append(pltpu.make_async_copy(src, g_buf.at[c * col_blocks + h], l_sem.at[3 + h]))
+    for copy in [struct_copy, dinv_copy] + own_copies:
+        copy.start()
 
     barrier = pltpu.get_barrier_semaphore()
     for d in range(1, nz):
@@ -64,14 +70,13 @@
         )
     for copy in g_nbr + panel_copies + g_sib:
         copy.start()
-    p_buf[z] = panels_ref[c]
-    for h in range(col_blocks):
-        g_buf[c * col_blocks + h] = ginv_ref[:, h * width:(h + 1) * width]
     for h in range(col_blocks):
         g_nbr[h].wait_recv()
         g_fwd[h].start()
     for copy in panel_copies + g_sib + g_fwd:
         copy.wait_recv()
+    for copy in own_copies + [struct_copy]:
+        copy.wait()
 
     for at in range(0, rows, keep):
         acc = jnp.zeros((keep, width), jnp.float32)
@@ -81,12 +86,13 @@
                 preferred_element_type=jnp.float32,
             )
         prod[at:at + keep, :] = acc
+        neg[at:at + keep, :] = -acc
 
     own_cols = pl.ds(pl.multiple_of(c * width, width), width)
     off_copies = []
     for at, ct in enumerate((nbr, dia, sib)):
         off_copies.append(
-            remote(prod.at[pl.ds(ct * keep, keep)], off_ref.at[:, own_cols], o_send.at[at], o_recv.at[at], z, ct)
+            remote(neg.at[pl.ds(ct * keep, keep)], off_ref.at[:, own_cols], o_send.at[at], o_recv.at[at], z, ct)
         )
 
     total = jnp.zeros((width, width), jnp.float32)
@@ -114,7 +120,7 @@
         )
     for copy in sum_copies + off_copies:
         copy.start()
-    off_ref[:, own_cols] = prod[pl.ds(c * keep, keep), :]
+    off_ref[:, own_cols] = neg[pl.ds(c * keep, keep), :]
 
     dinv_copy.wait()
     final = dinv_buf[...] + part[pl.ds(z * piece, piece), :]
@@ -143,10 +149,35 @@
     for d in range(nz):
         over_x[d].wait_recv()
         over_f[d].start()
-    for copy in off_copies + over_k + over_f:
+    for copy in off_copies:
         copy.wait_recv()
+    off_out = pltpu.make_async_copy(off_ref, off_hbm, l_sem.at[3 + col_blocks])
+    off_out.start()
+    for copy in over_k + over_f:
+        copy.wait_recv()
+    diag_out = pltpu.make_async_copy(diag_ref, diag_hbm, l_sem.at[4 + col_blocks])
+    diag_out.start()
     for copy in g_nbr + g_sib + g_fwd + panel_copies + off_copies + sum_copies + over_z + over_x + over_k + over_f:
         copy.wait_send()
+    off_out.wait()
+    diag_out.wait()
+
+
+def place_kernel(off_ref, diag_ref, off_out, diag_out, off_buf, diag_buf, sem):
+    step = off_ref.shape[0] // 2
+    parts = [(off_ref, off_out, off_buf, pl.ds(at * step, step)) for at in range(2)]
+    parts += [(diag_ref, diag_out, diag_buf, at) for at in range(diag_ref.shape[0])]
+    loads, stores = [], []
+    for n, (src, dst, buf, part) in enumerate(parts):
+        loads.append(pltpu.make_async_copy(src.at[part], buf.at[part], sem.at[0, n]))
+        stores.append(pltpu.make_async_copy(buf.at[part], dst.at[part], sem.at[1, n]))
+    for copy in loads:
+        copy.start()
+    for load, store in zip(loads, stores):
+        load.wait()
+        store.start()
+    for copy in stores:
+        copy.wait()
 
 
 def per_device(ginv, panels, structure, dinv):
@@ -156,37 +187,54 @@
     struct_count = structure.shape[1]
     col_blocks = cols // width
     piece = width // nz
-    vmem = pl.BlockSpec(memory_space=pltpu.VMEM)
+    hbm = pl.BlockSpec(memory_space=pl.ANY)
     dma = pltpu.SemaphoreType.DMA
+    out_shape = (
+        jax.ShapeDtypeStruct((rows // nc, super_count * width), jnp.float32),
+        jax.ShapeDtypeStruct((super_count, width, width), jnp.float32),
+    )
     off, diag = pl.pallas_call(
         functools.partial(invert_kernel, nz),
-        out_shape=(
-            jax.ShapeDtypeStruct((rows // nc, super_count * width), jnp.float32),
-            jax.ShapeDtypeStruct((super_count, width, width), jnp.float32),
-        ),
-        in_specs=[vmem, vmem, pl.BlockSpec(memory_space=pltpu.SMEM), pl.BlockSpec(memory_space=pl.ANY)],
-        out_specs=(vmem, vmem),
+        out_shape=out_shape,
+        in_specs=[hbm, hbm, hbm, hbm],
+        out_specs=(hbm, hbm),
         scratch_shapes=[
+            pltpu.SMEM((super_count, struct_count), jnp.int32),
             pltpu.VMEM((nc * col_blocks, rows, width), jnp.bfloat16),
             pltpu.VMEM((struct_count, width, width), jnp.bfloat16),
+            pltpu.VMEM((rows, width), jnp.float32),
             pltpu.VMEM((rows, width), jnp.float32),
             pltpu.VMEM((width, width), jnp.float32),
             pltpu.VMEM((nz - 1, piece, width), jnp.float32),
             pltpu.VMEM((piece, width), jnp.float32),
+            pltpu.VMEM((rows // nc, super_count * width), jnp.float32),
+            pltpu.VMEM((super_count, width, width), jnp.float32),
             dma((nz - 1,)), dma((nz - 1,)),
             dma((3, col_blocks)), dma((3, col_blocks)),
             dma((3,)), dma((3,)),
             dma((nz - 1,)), dma((nz - 1,)),
             dma((nz - 1,)), dma((nz - 1,)),
             dma((3, nz)), dma((3, nz)),
-            dma,
+            dma((5 + col_blocks,)),
         ],
         compiler_params=pltpu.CompilerParams(
             collective_id=0, has_side_effects=True, vmem_limit_bytes=VMEM_BYTES
         ),
         name="selected_inverse",
     )(ginv, panels, structure, dinv)
-    return -off, diag
+    return pl.pallas_call(
+        place_kernel,
+        out_shape=out_shape,
+        in_specs=[hbm, hbm],
+        out_specs=(hbm, hbm),
+        scratch_shapes=[
+            pltpu.VMEM((rows // nc, super_count * width), jnp.float32),
+            pltpu.VMEM((super_count, width, width), jnp.float32),
+            dma((2, 2 + super_count)),
+        ],
+        compiler_params=pltpu.CompilerParams(vmem_limit_bytes=VMEM_BYTES),
+        name="place_outputs",
+    )(off, diag)
 
 
 def solution(mesh):

time: 46.1 us -> 42.9 us (0.931)
  local copies, waits for them, and re-layouts: 4.95 us -> 0 us
  Pallas kernels: 39.3 us -> 42.1 us
  other arithmetic: 0.83 us -> 0 us
    unnamed x9 -> x0, local copies, waits for them, and re-layouts: 4.95 us -> none
    pallas_call x1 -> x2, Pallas kernels: 39.3 us -> 42.1 us  [the longest x1 39.9 us: per_device(): pl.pallas_call(functools.partial(invert_kernel, nz), out_shape=out_shape,...]
    neg x1 -> x0, other arithmetic: 0.83 us -> none  [per_device(): return (-off, diag)]
where the time goes in v2:
time: 42.9 us; the launch traced here: 42.7 us
  Pallas kernels  42.1 us (98%)
  between operations  0.64 us (1%)
    pallas_call x1, Pallas kernels, per_device(): pl.pallas_call(functools.partial(invert_kernel, nz), out_shape=out_shape,...  39.9 us
    pallas_call x1, Pallas kernels, per_device(): pl.pallas_call(place_kernel, out_shape=out_shape, in_specs=[hbm, hbm], ou...  2.19 us

profile of v2, /device:TPU:1, one launch (start us, length us, event | category | flops | bytes accessed | tf_op | source)
XLA Modules:
  0.0 42.7 jit_solution(6957096641092411588)
XLA Ops:
  0.6 39.9 %selected_inverse.1 = (f32[128,1024]{1,0:T(8,128)}, f32[4,256,256]{2,1,0:T(8,128)}) custom-call(bf16[512,512]{1,0:T(8,128)(2,1)} %ginv_ref.1, bf16[4,256,256]{2,1,0:T(8,128)(2,1)} %panels_ref.1, s32[4,4]{1,0:T(4,128)} %struct_hbm.1, f32[4,256,256]{2,1,0:T(8,128)} %dinv_ref.1), custom_call_target="tpu_custom_call" | custom-call | tf_op jit(solution)/shard_map/selected_inverse/pallas_call | solution.py:196
  40.5 2.2 %place_outputs.1 = (f32[128,1024]{1,0:T(8,128)}, f32[4,256,256]{2,1,0:T(8,128)}) custom-call(f32[128,1024]{1,0:T(8,128)} %get-tuple-element.4.off_ref, f32[4,256,256]{2,1,0:T(8,128)} %get-tuple-element.5.diag_ref), custom_call_target="tpu_custom_call" | custom-call | tf_op jit(solution)/shard_map/place_outputs/pallas_call | solution.py:225

commit v3 on v2

--- a/solution.py
+++ b/solution.py
@@ -9,11 +9,13 @@
 
 MESH = pl.DeviceIdType.MESH
 VMEM_BYTES = 60 * 1024 * 1024
+TILE = 16
+LEVELS = 32000.0
 
 
 def invert_kernel(
     nz, ginv_ref, panels_ref, struct_hbm, dinv_ref, off_hbm, diag_hbm,
-    struct_ref, g_buf, p_buf, prod, neg, part, rs_buf, dinv_buf, off_ref, diag_ref,
+    struct_ref, g_buf, p_buf, prod, neg, part, rs_buf, dinv_buf, off_ref, diag_ref, code,
     p_send, p_recv, g_send, g_recv, o_send, o_recv,
     r_send, r_recv, a_send, a_recv, h_send, h_recv, l_sem,
 ):
@@ -127,14 +129,32 @@
     for d in range(1, nz):
         sum_copies[d - 1].wait_recv()
         final += rs_buf[d - 1]
-    diag_ref[c, pl.ds(z * piece, piece), :] = final
+    coded = piece % TILE == 0
+
+    def at_piece(ct, j):
+        return code.at[ct, j] if coded else diag_ref.at[ct, pl.ds(j * piece, piece)]
+
+    def decode(ct, j):
+        if coded:
+            power = code[ct, j, piece:, :].astype(jnp.float32)[:1, :]
+            step = jnp.exp2(power) * (1.0 / LEVELS)
+            diag_ref[ct, pl.ds(j * piece, piece), :] = code[ct, j, :piece, :].astype(jnp.float32) * step
+
+    if coded:
+        largest = jnp.max(jnp.abs(final), axis=0, keepdims=True)
+        power = jnp.ceil(jnp.log2(jnp.maximum(largest, 1e-30)))
+        whole = jnp.round(final * (jnp.exp2(-power) * LEVELS)).astype(jnp.int32)
+        code[c, z, :piece, :] = whole.astype(jnp.int16)
+        below = jnp.broadcast_to(power, (TILE, width)).astype(jnp.int32)
+        code[c, z, piece:, :] = below.astype(jnp.int16)
+    else:
+        diag_ref[c, pl.ds(z * piece, piece), :] = final
 
     over_z, over_x, over_k, over_f = [], [], [], []
     for d in range(nz):
-        mine = diag_ref.at[c, pl.ds(zfrom(d) * piece, piece)]
-        theirs = diag_ref.at[nbr, pl.ds(zfrom(d) * piece, piece)]
+        mine, theirs = at_piece(c, zfrom(d)), at_piece(nbr, zfrom(d))
         if d > 0:
-            own = diag_ref.at[c, pl.ds(z * piece, piece)]
+            own = at_piece(c, z)
             over_z.append(remote(own, own, a_send.at[d - 1], a_recv.at[d - 1], zat(d), c))
         over_x.append(remote(mine, mine, h_send.at[0, d], h_recv.at[0, d], z, nbr))
         over_k.append(remote(mine, mine, h_send.at[1, d], h_recv.at[1, d], z, sib))
@@ -146,15 +166,19 @@
             over_z[d - 1].wait_recv()
         over_x[d].start()
         over_k[d].start()
+        decode(c, zfrom(d))
     for d in range(nz):
         over_x[d].wait_recv()
         over_f[d].start()
+        decode(nbr, zfrom(d))
     for copy in off_copies:
         copy.wait_recv()
     off_out = pltpu.make_async_copy(off_ref, off_hbm, l_sem.at[3 + col_blocks])
     off_out.start()
-    for copy in over_k + over_f:
-        copy.wait_recv()
+    for copies, ct in ((over_k, sib), (over_f, dia)):
+        for d in range(nz):
+            copies[d].wait_recv()
+            decode(ct, zfrom(d))
     diag_out = pltpu.make_async_copy(diag_ref, diag_hbm, l_sem.at[4 + col_blocks])
     diag_out.start()
     for copy in g_nbr + g_sib + g_fwd + panel_copies + off_copies + sum_copies + over_z + over_x + over_k + over_f:
@@ -209,6 +233,8 @@
             pltpu.VMEM((piece, width), jnp.float32),
             pltpu.VMEM((rows // nc, super_count * width), jnp.float32),
             pltpu.VMEM((super_count, width, width), jnp.float32),
+            pltpu.VMEM((super_count, nz, piece + TILE, width), jnp.int16)
+            if piece % TILE == 0 else pltpu.VMEM((8, 128), jnp.float32),
             dma((nz - 1,)), dma((nz - 1,)),
             dma((3, col_blocks)), dma((3, col_blocks)),
             dma((3,)), dma((3,)),

time: 42.9 us -> 40.6 us (0.946)
  Pallas kernels: 42.1 us -> 39.8 us
    pallas_call x1, Pallas kernels: 39.9 us -> 37.6 us  [per_device(): pl.pallas_call(functools.partial(invert_kernel, nz), out_shape=out_shape,...]
where the time goes in v3:
time: 40.6 us; the launch traced here: 40.4 us
  Pallas kernels  39.8 us (98%)
  between operations  0.64 us (2%)
    pallas_call x1, Pallas kernels, per_device(): pl.pallas_call(functools.partial(invert_kernel, nz), out_shape=out_shape,...  37.6 us
    pallas_call x1, Pallas kernels, per_device(): pl.pallas_call(place_kernel, out_shape=out_shape, in_specs=[hbm, hbm], ou...  2.19 us

profile of v3, /device:TPU:1, one launch (start us, length us, event | category | flops | bytes accessed | tf_op | source)
XLA Modules:
  0.0 40.4 jit_solution(9495330529662220388)
XLA Ops:
  0.6 37.6 %selected_inverse.1 = (f32[128,1024]{1,0:T(8,128)}, f32[4,256,256]{2,1,0:T(8,128)}) custom-call(bf16[512,512]{1,0:T(8,128)(2,1)} %ginv_ref.1, bf16[4,256,256]{2,1,0:T(8,128)(2,1)} %panels_ref.1, s32[4,4]{1,0:T(4,128)} %struct_hbm.1, f32[4,256,256]{2,1,0:T(8,128)} %dinv_ref.1), custom_call_target="tpu_custom_call" | custom-call | tf_op jit(solution)/shard_map/selected_inverse/pallas_call | solution.py:220
  38.2 2.2 %place_outputs.1 = (f32[128,1024]{1,0:T(8,128)}, f32[4,256,256]{2,1,0:T(8,128)}) custom-call(f32[128,1024]{1,0:T(8,128)} %get-tuple-element.4.off_ref, f32[4,256,256]{2,1,0:T(8,128)} %get-tuple-element.5.diag_ref), custom_call_target="tpu_custom_call" | custom-call | tf_op jit(solution)/shard_map/place_outputs/pallas_call | solution.py:251

commit v4 on v3

--- a/solution.py
+++ b/solution.py
@@ -150,6 +150,12 @@
     else:
         diag_ref[c, pl.ds(z * piece, piece), :] = final
 
+    placed = []
+
+    def place(n, ct):
+        placed.append(pltpu.make_async_copy(diag_ref.at[ct], diag_hbm.at[ct], l_sem.at[4 + col_blocks + n]))
+        placed[-1].start()
+
     over_z, over_x, over_k, over_f = [], [], [], []
     for d in range(nz):
         mine, theirs = at_piece(c, zfrom(d)), at_piece(nbr, zfrom(d))
@@ -167,24 +173,26 @@
         over_x[d].start()
         over_k[d].start()
         decode(c, zfrom(d))
+    place(0, c)
     for d in range(nz):
         over_x[d].wait_recv()
         over_f[d].start()
         decode(nbr, zfrom(d))
+    place(1, nbr)
     for copy in off_copies:
         copy.wait_recv()
     off_out = pltpu.make_async_copy(off_ref, off_hbm, l_sem.at[3 + col_blocks])
     off_out.start()
-    for copies, ct in ((over_k, sib), (over_f, dia)):
+    for n, copies, ct in ((2, over_k, sib), (3, over_f, dia)):
         for d in range(nz):
             copies[d].wait_recv()
             decode(ct, zfrom(d))
-    diag_out = pltpu.make_async_copy(diag_ref, diag_hbm, l_sem.at[4 + col_blocks])
-    diag_out.start()
+        place(n, ct)
     for copy in g_nbr + g_sib + g_fwd + panel_copies + off_copies + sum_copies + over_z + over_x + over_k + over_f:
         copy.wait_send()
     off_out.wait()
-    diag_out.wait()
+    for copy in placed:
+        copy.wait()
 
 
 def place_kernel(off_ref, diag_ref, off_out, diag_out, off_buf, diag_buf, sem):
@@ -241,7 +249,7 @@
             dma((nz - 1,)), dma((nz - 1,)),
             dma((nz - 1,)), dma((nz - 1,)),
             dma((3, nz)), dma((3, nz)),
-            dma((5 + col_blocks,)),
+            dma((8 + col_blocks,)),
         ],
         compiler_params=pltpu.CompilerParams(
             collective_id=0, has_side_effects=True, vmem_limit_bytes=VMEM_BYTES

time: 40.6 us -> 40.3 us (level)
  no operation moved by 1% of the time
where the time goes in v4:
time: 40.3 us; the launch traced here: 40.1 us
  Pallas kernels  39.5 us (98%)
  between operations  0.64 us (2%)
    pallas_call x1, Pallas kernels, per_device(): pl.pallas_call(functools.partial(invert_kernel, nz), out_shape=out_shape,...  37.3 us
    pallas_call x1, Pallas kernels, per_device(): pl.pallas_call(place_kernel, out_shape=out_shape, in_specs=[hbm, hbm], ou...  2.19 us

profile of v4, /device:TPU:1, one launch (start us, length us, event | category | flops | bytes accessed | tf_op | source)
XLA Modules:
  0.0 40.1 jit_solution(9408577628444555526)
XLA Ops:
  0.6 37.3 %selected_inverse.1 = (f32[128,1024]{1,0:T(8,128)}, f32[4,256,256]{2,1,0:T(8,128)}) custom-call(bf16[512,512]{1,0:T(8,128)(2,1)} %ginv_ref.1, bf16[4,256,256]{2,1,0:T(8,128)(2,1)} %panels_ref.1, s32[4,4]{1,0:T(4,128)} %struct_hbm.1, f32[4,256,256]{2,1,0:T(8,128)} %dinv_ref.1), custom_call_target="tpu_custom_call" | custom-call | tf_op jit(solution)/shard_map/selected_inverse/pallas_call | solution.py:228
  38.0 2.2 %place_outputs.1 = (f32[128,1024]{1,0:T(8,128)}, f32[4,256,256]{2,1,0:T(8,128)}) custom-call(f32[128,1024]{1,0:T(8,128)} %get-tuple-element.4.off_ref, f32[4,256,256]{2,1,0:T(8,128)} %get-tuple-element.5.diag_ref), custom_call_target="tpu_custom_call" | custom-call | tf_op jit(solution)/shard_map/place_outputs/pallas_call | solution.py:259
